TPU v7x, 32 devices: a whole 2x2x4 slice. The times are simulated.
32 devices in a mesh: layer: 4 (over y, x), row: 2 (over core), col: 4 (over z).
Axes of the slice: x: 2, y: 2, z: 4, core: 2. Of those that a mesh axis runs over, the one named last changes fastest.
Arguments:
- l_blocks: bfloat16 [4, 8, 256, 256], P('layer', ('row', 'col')), may hold values from -3 to 3
- l_ids: int32 [4, 8], P('layer'), may hold values from 0 to 127, as said below
- u_blocks: bfloat16 [4, 8, 256, 256], P('layer', ('row', 'col')), may hold values from -3 to 3
- u_ids: int32 [4, 8], P('layer'), may hold values from 0 to 127, as said below
- inv_upper: bfloat16 [8, 256, 256], replicated, as said below
- inv_lower: bfloat16 [8, 256, 256], replicated, as said below
- row_order: int32 [16], replicated, may hold values from 0 to 15, as said below
- col_order: int32 [16], replicated, may hold values from 0 to 15, as said below
- front_in: float32 [16, 16, 256, 256], P('row', 'col', 'layer'), may hold values from -6 to 6
- leaf_lower: bfloat16 [32, 1024, 1024], P(('layer', 'row', 'col')), may hold values from -6 to 6
- leaf_upper: bfloat16 [32, 1024, 1024], P(('layer', 'row', 'col')), may hold values from -0.1875 to 0.1875
- leaf_front: bfloat16 [32, 1024, 1024], P(('layer', 'row', 'col')), may hold values from -6 to 6
Outputs:
- front_out: float32 [16, 16, 256, 256], P('row', 'col', 'layer')
- leaf_out: bfloat16 [32, 1024, 1024], P(('layer', 'row', 'col'))
Inputs may be any that keep to these rules, and one draw needn't show every extreme that they name: `l_ids`: within a layer the ids are distinct; the entry at index r * 4 + c has i = row_order[r * 8 + p] for some p < 8. `u_ids`: within a layer the ids are distinct; the entry at index r * 4 + c has j = col_order[c * 4 + q] for some q < 4. `row_order`: A permutation of the tile rows. `col_order`: A permutation of the tile columns. `inv_upper`: each block is upper triangular with a positive diagonal. `inv_lower`: each block is lower triangular with a positive diagonal.
All inputs are finite; a program needn't handle non-finite values.
Results may differ from a plain program's by a relative error of at most 0.0095.
Values may be sent and summed in bfloat16 or wider, within the bound.
A program may use at most 128 MiB of HBM per device.

v0:
```python
import jax
import jax.numpy as jnp
from jax import lax
from jax.sharding import PartitionSpec as P


def place_all(carry, blocks, ids, wanted):
    matches = wanted[:, :, None] == ids[None, None, :]
    present = jnp.any(matches, axis=2)
    position = jnp.argmax(matches.astype(jnp.int32), axis=2)
    picked = blocks[position]
    return jnp.where(present[:, :, None, None], picked, carry)


def shards(
    l_blocks,
    l_ids,
    u_blocks,
    u_ids,
    inv_upper,
    inv_lower,
    row_order,
    col_order,
    front_in,
    leaf_lower,
    leaf_upper,
    leaf_front,
):
    tile = l_blocks.shape[-1]
    panel_count = inv_upper.shape[0]
    tiles_side = row_order.shape[0]
    rows_owned = front_in.shape[0]
    cols_owned = front_in.shape[1]
    grid_row = lax.axis_index("row")
    grid_col = lax.axis_index("col")
    row_count = lax.axis_size("row")
    col_count = lax.axis_size("col")
    lower_ids = l_ids[0]
    upper_ids = u_ids[0]
    place = grid_row * col_count + grid_col
    my_lower = lower_ids[place]
    my_upper = upper_ids[place]
    inv_u = lax.dynamic_index_in_dim(inv_upper, my_lower % panel_count, 0, keepdims=False)
    inv_l = lax.dynamic_index_in_dim(inv_lower, my_upper // tiles_side, 0, keepdims=False)
    lower = jnp.dot(l_blocks[0, 0], inv_u, preferred_element_type=jnp.float32).astype(jnp.bfloat16)
    upper = jnp.dot(inv_l, u_blocks[0, 0], preferred_element_type=jnp.float32).astype(jnp.bfloat16)
    owned_rows = lax.dynamic_slice_in_dim(row_order, grid_row * rows_owned, rows_owned)
    owned_cols = lax.dynamic_slice_in_dim(col_order, grid_col * cols_owned, cols_owned)
    panel = jnp.arange(panel_count, dtype=jnp.int32)
    want_lower = owned_rows[:, None] * panel_count + panel[None, :]
    want_upper = panel[:, None] * tiles_side + owned_cols[None, :]
    empty_lower = jnp.zeros((rows_owned, panel_count, tile, tile), jnp.bfloat16)
    empty_upper = jnp.zeros((panel_count, cols_owned, tile, tile), jnp.bfloat16)
    line_lower = lax.dynamic_slice_in_dim(lower_ids, grid_row * col_count, col_count)
    line_upper = lax.dynamic_slice_in_dim(upper_ids.reshape(row_count, col_count), grid_col, 1, 1)[
        :, 0
    ]
    low_sel = place_all(
        empty_lower, lax.all_gather(lower[None], "col", axis=0, tiled=True), line_lower, want_lower
    )
    up_sel = place_all(
        empty_upper, lax.all_gather(upper[None], "row", axis=0, tiled=True), line_upper, want_upper
    )
    schur = jnp.einsum("pkab,kqbc->pqac", low_sel, up_sel, preferred_element_type=jnp.float32)
    summed = lax.psum_scatter(
        schur.astype(jnp.bfloat16), "layer", scatter_dimension=2, tiled=True
    ).astype(jnp.float32)
    front_out = front_in - summed
    update = jnp.dot(leaf_lower[0], leaf_upper[0], preferred_element_type=jnp.float32)
    leaf_out = (leaf_front[0].astype(jnp.float32) - update).astype(jnp.bfloat16)[None]
    return (front_out, leaf_out)


def solution(mesh):
    return jax.shard_map(
        shards,
        mesh=mesh,
        in_specs=(
            P("layer", ("row", "col"), None, None),
            P("layer", None),
            P("layer", ("row", "col"), None, None),
            P("layer", None),
            P(),
            P(),
            P(),
            P(),
            P("row", "col", "layer", None),
            P(("layer", "row", "col"), None, None),
            P(("layer", "row", "col"), None, None),
            P(("layer", "row", "col"), None, None),
        ),
        out_specs=(P("row", "col", "layer", None), P(("layer", "row", "col"), None, None)),
        check_vma=False,
    )
```

profile of v0, /device:TPU:0, one launch (start us, length us, event | category | flops | bytes accessed | tf_op | source)
XLA Modules:
  0.0 139.0 jit_solution(16265622520289946342)
XLA Ops:
  7.2 1.4 %constant_dynamic-slice_fusion = (s32[1,1]{1,0:T(1,128)}, s32[1,1]{1,0:T(1,128)}) fusion(s32[1,8]{1,0:T(1,128)} %param.13, s32[]{:T(128)S(6)} %select_n.58, s32[1,8]{1,0:T(1,128)} %param.15), kind=kLoop, calls=%fused_computation.39 | loop fusion | bytes 20 | tf_op jit(solution)/shard_map/dynamic_slice | solution.py:41
  13.2 0.5 broadcast.64
  13.7 1.3 reduce.43
  15.0 0.1 reshape_squeeze.3
  15.1 0.7 dynamic_slice.25
  15.9 0.2 fusion.31
  16.1 0.7 fusion.28
  16.9 0.7 fusion.32
  17.6 0.7 dynamic-slice_multiply_fusion
  18.4 0.7 fusion.27
  19.1 1.2 fusion.20
  20.3 17.4 %all-gather.1 = bf16[1024,256]{0,1:T(8,128)(2,1)S(1)} all-gather(bf16[256,256]{0,1:T(8,128)(2,1)S(1)} %fusion.20), channel_id=3, replica_groups=mesh['layer'=4,'row'=2,'col'=4] {'col'}, dimensions={0}, use_global_device_ids=true | all-gather | bytes 655360 | tf_op jit(solution)/shard_map/all_gather | solution.py:59
  37.7 0.2 copy.37
  38.0 1.2 convolution_convert_fusion.1
  39.2 2.0 %all-gather = bf16[512,256]{1,0:T(8,128)(2,1)S(1)} all-gather(bf16[256,256]{1,0:T(8,128)(2,1)S(1)} %convolution_convert_fusion.1), channel_id=2, replica_groups=mesh['layer'=4,'row'=2,'col'=4] {'row'}, dimensions={0}, use_global_device_ids=true | all-gather | bytes 393216 | tf_op jit(solution)/shard_map/all_gather | solution.py:62
  41.3 0.1 copy.26
  41.4 5.3 %gather_fusion.1 = bf16[64,256,256]{2,1,0:T(8,128)(2,1)} fusion(bf16[4,256,256]{2,1,0:T(8,128)(2,1)S(1)} %bitcast.53, s32[1024]{0:T(1024)S(1)} %pad_clamp_fusion), kind=kCustom, calls=%fused_computation.1 | custom fusion | bytes 16777472 | tf_op jit(solution)/shard_map/gather | solution.py:11
  46.7 2.8 %gather_fusion = bf16[32,256,256]{2,1,0:T(8,128)(2,1)} fusion(bf16[2,256,256]{2,1,0:T(8,128)(2,1)S(1)} %bitcast.54, s32[1024]{0:T(1024)S(1)} %pad_clamp_fusion.1), kind=kCustom, calls=%fused_computation | custom fusion | bytes 8388736 | tf_op jit(solution)/shard_map/gather | solution.py:11
  49.5 14.4 %fusion.4 = bf16[8,4,256,256]{2,3,0,1:T(8,128)(2,1)} fusion(bf16[8,8,256,256]{3,2,1,0:T(8,128)(2,1)} %bitcast.55, pred[8,8]{1,0:T(8,128)(4,1)S(1)} %compare_reduce_fusion, bf16[8,4,256,256]{3,2,1,0:T(8,128)(2,1)} %bitcast.56, pred[8,4]{1,0:T(8,128)(4,1)S(1)} %copy.26), kind=kOutput, calls=%fused_computation.7 | convolution fusion | flops 8598323200 | bytes 16777312 | tf_op jit(solution)/shard_map/pkab,kqbc->pqac/dot_general | solution.py:64
  63.9 8.0 %copy.30 = bf16[8,4,256,256]{3,0,1,2:T(8,128)(2,1)} copy(bf16[8,4,256,256]{2,3,0,1:T(8,128)(2,1)} %fusion.4) | data formatting | bytes 8388608 | tf_op jit(solution)/shard_map/convert_element_type | solution.py:66
  71.9 5.9 %fusion.12 = bf16[1,1024,1024]{2,1,0:T(8,128)(2,1)} fusion(bf16[1,1024,1024]{2,1,0:T(8,128)(2,1)} %param.23, bf16[1,1024,1024]{2,1,0:T(8,128)(2,1)S(1)} %copy-done, bf16[1,1024,1024]{2,1,0:T(8,128)(2,1)} %param.21), kind=kOutput, calls=%fused_computation.13 | convolution fusion | flops 2150629376 | bytes 8388608 | tf_op jit(solution)/shard_map/dot_general | solution.py:69
  77.7 48.7 %reduce-scatter.2.cloned.1.call-done = bf16[8,4,64,256]{3,0,1,2:T(8,128)(2,1)} async-done(((bf16[8,4,256,256]{3,0,1,2:T(8,128)(2,1)}), bf16[8,4,64,256]{3,0,1,2:T(8,128)(2,1)}) %reduce-scatter.2.cloned.1.call-update) | async-done | bytes 1048592 | tf_op jit(solution)/shard_map/reduce_scatter | solution.py:65
  126.5 3.1 %copy_subtract_fusion = f32[8,4,64,256]{3,0,1,2:T(8,128)S(1)} fusion(f32[8,4,64,256]{3,2,1,0:T(8,128)} %param.20, bf16[8,4,64,256]{3,0,1,2:T(8,128)(2,1)} %reduce-scatter.2.cloned.1.call-done), kind=kLoop, calls=%fused_computation.17 | loop fusion | flops 1048576 | bytes 5242880 | tf_op jit(solution)/shard_map/sub | solution.py:68
  129.6 2.5 %copy.32 = f32[8,4,64,256]{3,2,1,0:T(8,128)} copy(f32[8,4,64,256]{3,0,1,2:T(8,128)S(1)} %copy_subtract_fusion) | data formatting | bytes 4194304
  (16 shorter events, 0.6 us)
Async XLA Ops:
  7.2 64.7 %copy-start = (bf16[1,1024,1024]{2,1,0:T(8,128)(2,1)S(1)}, bf16[1,1024,1024]{2,1,0:T(8,128)(2,1)}, u32[]{:S(2)}) copy-start(bf16[1,1024,1024]{2,1,0:T(8,128)(2,1)} %param.22) | copy-start | bytes 6291460
  7.2 119.3 %reduce-scatter.2.cloned.1.call-start = ((), (), s32[]{:S(2)}) async-start(), calls=%async_computation.1 | async-start | bytes 5242880 | tf_op jit(solution)/shard_map/reduce_scatter | solution.py:65
Sparse Core Ops, SparseCore 0:
  72.0 54.4 reduce-scatter.1
where the time goes:
time: 139 us
  waiting for transfers between devices  48.8 us (35%)
  local copies, waits for them, and re-layouts  22.7 us (16%)
  matrix products  22.6 us (16%)
  blocking collectives  19.4 us (14%)
  between operations  18.7 us (13%)
  other arithmetic  6.81 us (5%)
    reduce_scatter x1, waiting for transfers between devices, shards(): lax.psum_scatter(schur.astype(jnp.bfloat16), 'layer', scatter_dimension=2...  48.7 us
    all_gather x1, blocking collectives, shards(): lax.all_gather(lower[None], 'col', axis=0, tiled=True)  17.4 us
    dot_general x1, matrix products, shards(): jnp.einsum('pkab,kqbc->pqac', low_sel, up_sel, preferred_element_type=jnp...  14.4 us
    gather x2, local copies, waits for them, and re-layouts, place_all(): picked = blocks[position]  8.03 us
    convert_element_type x1, local copies, waits for them, and re-layouts, shards(): schur.astype(jnp.bfloat16)  7.95 us
    dot_general x1, matrix products, shards(): jnp.dot(leaf_lower[0], leaf_upper[0], preferred_element_type=jnp.float32)  5.87 us
    sub x1, other arithmetic, shards(): front_out = front_in - summed  3.09 us
    unnamed x4, local copies, waits for them, and re-layouts  3.06 us
  transfers between devices with their start and end apart: 1, of which 1 were waited for; matrix products, arithmetic and copies ran while one was open for 4% of the time, Pallas kernels for 0%

commit v1 on v0

v1 whole, which is shorter than its diff:
```python
import functools

import jax
import jax.numpy as jnp
from jax import lax
from jax.experimental import pallas as pl
from jax.experimental.pallas import tpu as pltpu
from jax.sharding import PartitionSpec as P

MESH = pl.DeviceIdType.MESH
LEAF_ROWS = 512
LEAF_COLS = 256


def exchange(
    sizes,
    l_ids_sm, u_ids_sm, l_ids_hbm, u_ids_hbm, l_hbm, u_hbm, inv_u_hbm, inv_l_hbm,
    front_hbm, ll_hbm, lu_hbm, lf_hbm,
    low_all, up_all, l_ids_all, u_ids_all, front_v, leaf_v,
    l_v, u_v, inv_u, inv_l, lower, upper, ll, lu, lf,
    loc, low_recv, low_send, line_send, up_recv, up_send, up_fwd, ids_recv, ids_send,
):
    n_layer, n_row, n_col, tiles_side = sizes
    lay = lax.axis_index("layer")
    row = lax.axis_index("row")
    col = lax.axis_index("col")
    panels = inv_u.shape[0]
    high = low_all.shape[2]

    def layer_at(t):
        return lax.rem(lay + t, n_layer)

    def row_at(t):
        return lax.rem(row + t, n_row)

    local = [
        (inv_u_hbm, inv_u), (l_hbm.at[0, 0], l_v), (inv_l_hbm, inv_l), (u_hbm.at[0, 0], u_v),
        (ll_hbm.at[0], ll), (lu_hbm.at[0], lu), (lf_hbm.at[0], lf), (front_hbm, front_v),
        (l_ids_hbm, l_ids_all.at[lay]), (u_ids_hbm, u_ids_all.at[lay]),
    ]
    local = [pltpu.make_async_copy(src, dst, loc.at[i]) for i, (src, dst) in enumerate(local)]
    for copy in local:
        copy.start()

    barrier = pltpu.get_barrier_semaphore()

    def greet(device):
        pl.semaphore_signal(barrier, inc=1, device_id=device, device_id_type=MESH)

    for t in range(1, n_layer):
        greet({"layer": layer_at(t)})
    for t in range(1, n_row):
        greet({"row": row_at(t)})

    @pl.when(col + 1 < n_col)
    def _():
        greet({"col": col + 1})

    @pl.when(col > 0)
    def _():
        greet({"col": col - 1})

    def low_copy(src, s, l, sem, device):
        return pltpu.make_async_remote_copy(
            src_ref=src, dst_ref=low_all.at[s, l], send_sem=sem, recv_sem=low_recv.at[s, l],
            device_id=device, device_id_type=MESH)

    def up_copy(src, l, sem, device):
        return pltpu.make_async_remote_copy(
            src_ref=src, dst_ref=up_all.at[row, l], send_sem=sem, recv_sem=up_recv.at[row, l],
            device_id=device, device_id_type=MESH)

    def low_rows(l):
        return lower.at[pl.ds(pl.multiple_of(l * high, high), high)]

    def right(s, l):
        return low_copy(low_all.at[s, l], s, l, line_send.at[0, s, l], {"col": col + 1})

    def left(s, l):
        return low_copy(low_all.at[s, l], s, l, line_send.at[1, s, l], {"col": col - 1})

    def plane(t):
        l = layer_at(t)
        return low_copy(low_rows(l), col, lay, low_send.at[l], {"layer": l})

    def up_plane(t):
        l = layer_at(t)
        return up_copy(upper, lay, up_send.at[l], {"layer": l})

    def up_row(l, t):
        r = row_at(t)
        return up_copy(up_all.at[row, l], l, up_fwd.at[r, l], {"row": r})

    def ids_copy(which, src, dst, t):
        l = layer_at(t)
        return pltpu.make_async_remote_copy(
            src_ref=src, dst_ref=dst.at[lay], send_sem=ids_send.at[which, l],
            recv_sem=ids_recv.at[which, lay], device_id={"layer": l}, device_id_type=MESH)

    def low_arrived(s, l):
        low_copy(low_all.at[s, l], s, l, low_send.at[0], {"layer": layer_at(1)}).wait_recv()

    def leaf(first, last):
        per = ll.shape[0] // LEAF_ROWS

        def body(i, carry):
            rows = pl.ds(pl.multiple_of(lax.rem(i, per) * LEAF_ROWS, LEAF_ROWS), LEAF_ROWS)
            cols = pl.ds(pl.multiple_of((i // per) * LEAF_COLS, LEAF_COLS), LEAF_COLS)
            update = jnp.dot(ll[rows, :], lu[:, cols], preferred_element_type=jnp.float32)
            leaf_v[rows, cols] = (lf[rows, cols].astype(jnp.float32) - update).astype(leaf_v.dtype)
            return carry

        lax.fori_loop(first, last, body, 0)

    n_leaf = (ll.shape[0] // LEAF_ROWS) * (lu.shape[1] // LEAF_COLS)
    place = row * n_col + col

    local[0].wait()
    local[1].wait()
    lower[...] = jnp.dot(
        l_v[...], inv_u[l_ids_sm[0, place] % panels], preferred_element_type=jnp.float32
    ).astype(lower.dtype)
    low_all[col, lay] = low_rows(lay)[...]

    on_line = (col + 1 < n_col).astype(jnp.int32) + (col > 0).astype(jnp.int32)
    pl.semaphore_wait(barrier, n_layer - 1 + n_row - 1 + on_line)

    for t in range(1, n_layer):
        plane(t).start()

    def pass_on(s, l, go_right, go_left):
        if go_right:
            @pl.when(col + 1 < n_col)
            def _():
                right(s, l).start()
        if go_left:
            @pl.when(col > 0)
            def _():
                left(s, l).start()

    pass_on(col, lay, True, True)

    local[2].wait()
    local[3].wait()
    upper[...] = jnp.dot(
        inv_l[u_ids_sm[0, place] // tiles_side], u_v[...], preferred_element_type=jnp.float32
    ).astype(upper.dtype)
    up_all[row, lay] = upper[...]
    for t in range(1, n_layer):
        up_plane(t).start()
    for t in range(1, n_row):
        up_row(lay, t).start()
    for t in range(1, n_layer):
        ids_copy(0, l_ids_hbm, l_ids_all, t).start()
        ids_copy(1, u_ids_hbm, u_ids_all, t).start()

    for copy in local[4:]:
        copy.wait()

    for t in range(1, n_layer):
        l = layer_at(t)
        low_arrived(col, l)
        pass_on(col, l, True, True)
    leaf(0, n_leaf // 4)

    for d in range(1, n_col):
        for t in range(n_layer):
            l = layer_at(t)

            @pl.when(col - d >= 0)
            def _():
                low_arrived(col - d, l)
                pass_on(col - d, l, True, False)

            @pl.when(col + d < n_col)
            def _():
                low_arrived(col + d, l)
                pass_on(col + d, l, False, True)

        if d == 1:
            leaf(n_leaf // 4, n_leaf)
        if d == max(1, n_col - 2):
            for t in range(1, n_layer):
                l = layer_at(t)
                up_copy(upper, l, up_send.at[l], {"layer": l}).wait_recv()
                for u in range(1, n_row):
                    up_row(l, u).start()

    for t in range(1, n_row):
        for l in range(n_layer):
            r = row_at(t)
            pltpu.make_async_remote_copy(
                src_ref=upper, dst_ref=up_all.at[r, l], send_sem=up_fwd.at[r, l],
                recv_sem=up_recv.at[r, l], device_id={"row": r}, device_id_type=MESH).wait_recv()
            up_row(l, t).wait_send()
    for t in range(1, n_layer):
        plane(t).wait_send()
        up_plane(t).wait_send()
        l = layer_at(t)
        for which, src, dst in ((0, l_ids_hbm, l_ids_all), (1, u_ids_hbm, u_ids_all)):
            ids_copy(which, src, dst, t).wait_send()
            pltpu.make_async_remote_copy(
                src_ref=src, dst_ref=dst.at[l], send_sem=ids_send.at[which, l],
                recv_sem=ids_recv.at[which, l], device_id={"layer": l},
                device_id_type=MESH).wait_recv()
    for d in range(n_col):
        for l in range(n_layer):
            @pl.when((col - d >= 0) & (col + 1 < n_col))
            def _():
                right(col - d, l).wait_send()

            @pl.when((col + d < n_col) & (col > 0))
            def _():
                left(col + d, l).wait_send()


def finish(
    sizes,
    l_ids, u_ids, row_order, col_order, low_all, up_all, front_v, leaf_v,
    front_out, leaf_out, acc, sem,
):
    n_layer, n_row, n_col, tiles_side, panels = sizes
    row = lax.axis_index("row")
    col = lax.axis_index("col")
    rows_owned, cols_owned = acc.shape[0], acc.shape[1]
    leaf_copy = pltpu.make_async_copy(leaf_v, leaf_out.at[0], sem.at[0])
    leaf_copy.start()
    acc[...] = front_v[...]

    def find(order, start, count, value):
        at = jnp.int32(0)
        for a in range(count):
            at = jnp.where(order[start + a] == value, jnp.int32(a), at)
        return at

    for l in range(n_layer):
        for m2 in range(n_row):
            uid = u_ids[l, 0, m2 * n_col + col]
            for m in range(n_col):
                lid = l_ids[l, 0, row * n_col + m]

                @pl.when(lid % panels == uid // tiles_side)
                def _():
                    p = find(row_order, row * rows_owned, rows_owned, lid // panels)
                    q = find(col_order, col * cols_owned, cols_owned, uid % tiles_side)
                    acc[p, q] = acc[p, q] - jnp.dot(
                        low_all[m, l], up_all[m2, l], preferred_element_type=jnp.float32)

    front_copy = pltpu.make_async_copy(acc, front_out, sem.at[1])
    front_copy.start()
    front_copy.wait()
    leaf_copy.wait()


def shards(
    sizes,
    l_blocks, l_ids, u_blocks, u_ids, inv_upper, inv_lower, row_order, col_order,
    front_in, leaf_lower, leaf_upper, leaf_front,
):
    n_layer, n_row, n_col = sizes
    tile = l_blocks.shape[-1]
    high = front_in.shape[2]
    n_ids = l_ids.shape[1]
    tiles_side = row_order.shape[0]
    bf16, i32 = jnp.bfloat16, jnp.int32
    vmem = pl.BlockSpec(memory_space=pltpu.VMEM)
    smem = pl.BlockSpec(memory_space=pltpu.SMEM)
    any_ = pl.BlockSpec(memory_space=pl.ANY)
    hbm = pl.BlockSpec(memory_space=pltpu.HBM)
    dma = pltpu.SemaphoreType.DMA
    leaf_shape = leaf_front.shape[1:]
    low_all, up_all, l_all, u_all, front_v, leaf_v = pl.pallas_call(
        functools.partial(exchange, (n_layer, n_row, n_col, tiles_side)),
        name="exchange",
        out_shape=(
            pltpu.VMEM((n_col, n_layer, high, tile), bf16),
            pltpu.VMEM((n_row, n_layer, tile, tile), bf16),
            jax.ShapeDtypeStruct((n_layer, 1, n_ids), i32),
            jax.ShapeDtypeStruct((n_layer, 1, n_ids), i32),
            pltpu.VMEM(front_in.shape, front_in.dtype),
            pltpu.VMEM(leaf_shape, bf16),
        ),
        in_specs=[smem, smem] + [hbm] * 10,
        out_specs=(vmem, vmem, any_, any_, vmem, vmem),
        scratch_shapes=[
            pltpu.VMEM((tile, tile), bf16),
            pltpu.VMEM((tile, tile), bf16),
            pltpu.VMEM(inv_upper.shape, bf16),
            pltpu.VMEM(inv_lower.shape, bf16),
            pltpu.VMEM((tile, tile), bf16),
            pltpu.VMEM((tile, tile), bf16),
            pltpu.VMEM(leaf_lower.shape[1:], bf16),
            pltpu.VMEM(leaf_upper.shape[1:], bf16),
            pltpu.VMEM(leaf_shape, bf16),
            dma((10,)),
            dma((n_col, n_layer)),
            dma((n_layer,)),
            dma((2, n_col, n_layer)),
            dma((n_row, n_layer)),
            dma((n_layer,)),
            dma((n_row, n_layer)),
            dma((2, n_layer)),
            dma((2, n_layer)),
        ],
        compiler_params=pltpu.CompilerParams(
            collective_id=0, has_side_effects=True, vmem_limit_bytes=28 * 2**20),
    )(l_ids, u_ids, l_ids, u_ids, l_blocks, u_blocks, inv_upper, inv_lower,
      front_in, leaf_lower, leaf_upper, leaf_front)
    return pl.pallas_call(
        functools.partial(finish, (n_layer, n_row, n_col, tiles_side, inv_upper.shape[0])),
        name="finish",
        out_shape=(
            jax.ShapeDtypeStruct(front_in.shape, front_in.dtype),
            jax.ShapeDtypeStruct(leaf_front.shape, bf16),
        ),
        in_specs=[smem] * 4 + [vmem] * 4,
        out_specs=(any_, any_),
        scratch_shapes=[pltpu.VMEM(front_in.shape, front_in.dtype), dma((2,))],
        compiler_params=pltpu.CompilerParams(vmem_limit_bytes=28 * 2**20),
    )(l_all, u_all, row_order, col_order, low_all, up_all, front_v, leaf_v)


def solution(mesh):
    sizes = (mesh.shape["layer"], mesh.shape["row"], mesh.shape["col"])
    leaf = P(("layer", "row", "col"), None, None)
    return jax.shard_map(
        functools.partial(shards, sizes),
        mesh=mesh,
        in_specs=(
            P("layer", ("row", "col"), None, None),
            P("layer", None),
            P("layer", ("row", "col"), None, None),
            P("layer", None),
            P(),
            P(),
            P(),
            P(),
            P("row", "col", "layer", None),
            leaf,
            leaf,
            leaf,
        ),
        out_specs=(P("row", "col", "layer", None), leaf),
        check_vma=False,
    )
```

time: 139 us -> 38.8 us (0.28)
  waiting for transfers between devices: 48.8 us -> 0 us
  Pallas kernels: 0 us -> 25.8 us
  matrix products: 22.6 us -> 0 us
  blocking collectives: 19.4 us -> 0 us
  between operations: 18.7 us -> 0.68 us
  local copies, waits for them, and re-layouts: 22.7 us -> 11.9 us
  other arithmetic: 6.81 us -> 0 us
    reduce_scatter x1 -> x0, waiting for transfers between devices: 48.7 us -> none  [shards(): lax.psum_scatter(schur.astype(jnp.bfloat16), 'layer', scatter_dimension=2...]
    pallas_call x0 -> x2, Pallas kernels: none -> 25.8 us  [the longest x1 22.9 us: shards(): pl.pallas_call(functools.partial(exchange, (n_layer, n_row, n_col, tiles_...]
    dot_general x4 -> x0, matrix products: 22.6 us -> none  [the longest x1 14.4 us: shards(): jnp.einsum('pkab,kqbc->pqac', low_sel, up_sel, preferred_element_type=jnp...]
    all_gather x2 -> x0, blocking collectives: 19.4 us -> none  [the longest x1 17.4 us: shards(): lax.all_gather(lower[None], 'col', axis=0, tiled=True)]
    unnamed x4 -> x24, local copies, waits for them, and re-layouts: 3.06 us -> 11.9 us
    gather x2 -> x0, local copies, waits for them, and re-layouts: 8.03 us -> none  [place_all(): picked = blocks[position]]
    convert_element_type x1 -> x0, local copies, waits for them, and re-layouts: 7.95 us -> none  [shards(): schur.astype(jnp.bfloat16)]
    sub x1 -> x0, other arithmetic: 3.09 us -> none  [shards(): front_out = front_in - summed]
  transfers between devices with their start and end apart: 1 -> 0, of which waited for: 1 -> 0; matrix products, arithmetic and copies ran while one was open for 4% -> 0% of each run, Pallas kernels for 0% -> 0%
where the time goes in v1:
time: 38.8 us; the launch traced here: 38.4 us
  Pallas kernels  25.8 us (66%)
  local copies, waits for them, and re-layouts  11.9 us (31%)
  between operations  0.68 us (2%)
    pallas_call x1, Pallas kernels, shards(): pl.pallas_call(functools.partial(exchange, (n_layer, n_row, n_col, tiles_...  22.9 us
    unnamed x24, local copies, waits for them, and re-layouts  11.9 us
    pallas_call x1, Pallas kernels, shards(): pl.pallas_call(functools.partial(finish, (n_layer, n_row, n_col, tiles_si...  2.96 us

profile of v1, /device:TPU:0, one launch (start us, length us, event | category | flops | bytes accessed | tf_op | source)
XLA Modules:
  0.0 38.4 jit_solution(3130740679590361844)
XLA Ops:
  0.6 0.0 copy-start
  0.6 1.6 %copy-done = f32[8,4,64,256]{3,2,1,0:T(8,128)S(1)} copy-done((f32[8,4,64,256]{3,2,1,0:T(8,128)S(1)}, f32[8,4,64,256]{3,2,1,0:T(8,128)}, u32[]{:S(2)}) %copy-start) | copy-done | bytes 2097176
  2.2 0.0 copy-start.1
  2.2 1.6 %copy-done.1 = bf16[1,1024,1024]{2,1,0:T(8,128)(2,1)S(1)} copy-done((bf16[1,1024,1024]{2,1,0:T(8,128)(2,1)S(1)}, bf16[1,1024,1024]{2,1,0:T(8,128)(2,1)}, u32[]{:S(2)}) %copy-start.1) | copy-done | bytes 2097176
  3.8 0.0 copy-start.2
  3.8 1.6 %copy-done.2 = bf16[1,1024,1024]{2,1,0:T(8,128)(2,1)S(1)} copy-done((bf16[1,1024,1024]{2,1,0:T(8,128)(2,1)S(1)}, bf16[1,1024,1024]{2,1,0:T(8,128)(2,1)}, u32[]{:S(2)}) %copy-start.2) | copy-done | bytes 2097176
  5.4 0.0 copy-start.3
  5.4 1.6 %copy-done.3 = bf16[1,1024,1024]{2,1,0:T(8,128)(2,1)S(1)} copy-done((bf16[1,1024,1024]{2,1,0:T(8,128)(2,1)S(1)}, bf16[1,1024,1024]{2,1,0:T(8,128)(2,1)}, u32[]{:S(2)}) %copy-start.3) | copy-done | bytes 2097176
  7.0 0.0 copy-start.4
  7.0 1.2 %copy-done.4 = bf16[8,256,256]{2,1,0:T(8,128)(2,1)S(1)} copy-done((bf16[8,256,256]{2,1,0:T(8,128)(2,1)S(1)}, bf16[8,256,256]{2,1,0:T(8,128)(2,1)}, u32[]{:S(2)}) %copy-start.4) | copy-done | bytes 1048600
  8.2 0.0 copy-start.5
  8.2 1.2 %copy-done.5 = bf16[8,256,256]{2,1,0:T(8,128)(2,1)S(1)} copy-done((bf16[8,256,256]{2,1,0:T(8,128)(2,1)S(1)}, bf16[8,256,256]{2,1,0:T(8,128)(2,1)}, u32[]{:S(2)}) %copy-start.5) | copy-done | bytes 1048600
  9.5 0.0 copy-start.6
  9.5 0.9 %copy-done.6 = bf16[1,1,256,256]{3,2,1,0:T(8,128)(2,1)S(1)} copy-done((bf16[1,1,256,256]{3,2,1,0:T(8,128)(2,1)S(1)}, bf16[1,1,256,256]{3,2,1,0:T(8,128)(2,1)}, u32[]{:S(2)}) %copy-start.6) | copy-done | bytes 131096
  10.4 0.0 copy-start.7
  10.4 0.9 %copy-done.7 = bf16[1,1,256,256]{3,2,1,0:T(8,128)(2,1)S(1)} copy-done((bf16[1,1,256,256]{3,2,1,0:T(8,128)(2,1)S(1)}, bf16[1,1,256,256]{3,2,1,0:T(8,128)(2,1)}, u32[]{:S(2)}) %copy-start.7) | copy-done | bytes 131096
  11.3 0.0 copy-start.8
  11.3 0.7 %copy-done.8 = s32[1,8]{1,0:T(1,128)S(1)} copy-done((s32[1,8]{1,0:T(1,128)S(1)}, s32[1,8]{1,0:T(1,128)}, u32[]{:S(2)}) %copy-start.8) | copy-done | bytes 56
  11.9 0.0 copy-start.9
  11.9 0.7 %copy-done.9 = s32[1,8]{1,0:T(1,128)S(1)} copy-done((s32[1,8]{1,0:T(1,128)S(1)}, s32[1,8]{1,0:T(1,128)}, u32[]{:S(2)}) %copy-start.9) | copy-done | bytes 56
  12.6 22.9 %exchange.1 = (bf16[4,4,64,256]{3,2,1,0:T(8,128)(2,1)S(1)}, bf16[2,4,256,256]{3,2,1,0:T(8,128)(2,1)S(1)}, s32[4,1,8]{2,1,0:T(1,128)S(1)}, s32[4,1,8]{2,1,0:T(1,1...) custom-call(s32[1,8]{1,0:T(1,128)S(1)} %copy-done.8, s32[1,8]{1,0:T(1,128)S(1)} %copy-done.9, ...), custom_call_target="tpu_custom_call" | custom-call | tf_op jit(solution)/shard_map/exchange/pallas_call | solution.py:272
  35.4 0.0 copy-done.10
  35.5 0.0 copy-done.11
  35.5 3.0 %finish.1 = (f32[8,4,64,256]{3,2,1,0:T(8,128)}, bf16[1,1024,1024]{2,1,0:T(8,128)(2,1)}) custom-call(s32[4,1,8]{2,1,0:T(1,128)S(1)} %get-tuple-element.8.l_ids, s32[4,1,8]{2,1,0:T(1,128)S(1)} %get-tuple-element.9.u_ids, s32[16]{0:T(128)S(1)} %copy-done.10, s32[16]{0:T(128)S(1)} %copy-done.11, bf16[4,4,64,256]{3,2,1,0:T(8,128)(2,1)S(1)} %get-tuple-element.10.low_all, ...), custom_call_target="tpu_custom_call" | custom-call | tf_op jit(solution)/shard_map/finish/pallas_call | solution.py:309
  (2 shorter events, 0.0 us)
Async XLA Ops:
  0.6 1.6 %copy-start = (f32[8,4,64,256]{3,2,1,0:T(8,128)S(1)}, f32[8,4,64,256]{3,2,1,0:T(8,128)}, u32[]{:S(2)}) copy-start(f32[8,4,64,256]{3,2,1,0:T(8,128)} %front_hbm.1) | copy-start | bytes 6291460
  2.2 1.6 %copy-start.1 = (bf16[1,1024,1024]{2,1,0:T(8,128)(2,1)S(1)}, bf16[1,1024,1024]{2,1,0:T(8,128)(2,1)}, u32[]{:S(2)}) copy-start(bf16[1,1024,1024]{2,1,0:T(8,128)(2,1)} %ll_hbm.1) | copy-start | bytes 6291460
  3.8 1.6 %copy-start.2 = (bf16[1,1024,1024]{2,1,0:T(8,128)(2,1)S(1)}, bf16[1,1024,1024]{2,1,0:T(8,128)(2,1)}, u32[]{:S(2)}) copy-start(bf16[1,1024,1024]{2,1,0:T(8,128)(2,1)} %lu_hbm.1) | copy-start | bytes 6291460
  5.4 1.6 %copy-start.3 = (bf16[1,1024,1024]{2,1,0:T(8,128)(2,1)S(1)}, bf16[1,1024,1024]{2,1,0:T(8,128)(2,1)}, u32[]{:S(2)}) copy-start(bf16[1,1024,1024]{2,1,0:T(8,128)(2,1)} %lf_hbm.1) | copy-start | bytes 6291460
  7.0 1.2 %copy-start.4 = (bf16[8,256,256]{2,1,0:T(8,128)(2,1)S(1)}, bf16[8,256,256]{2,1,0:T(8,128)(2,1)}, u32[]{:S(2)}) copy-start(bf16[8,256,256]{2,1,0:T(8,128)(2,1)} %inv_u_hbm.1) | copy-start | bytes 3145732
  8.2 1.2 %copy-start.5 = (bf16[8,256,256]{2,1,0:T(8,128)(2,1)S(1)}, bf16[8,256,256]{2,1,0:T(8,128)(2,1)}, u32[]{:S(2)}) copy-start(bf16[8,256,256]{2,1,0:T(8,128)(2,1)} %inv_l_hbm.1) | copy-start | bytes 3145732
  9.5 0.9 %copy-start.6 = (bf16[1,1,256,256]{3,2,1,0:T(8,128)(2,1)S(1)}, bf16[1,1,256,256]{3,2,1,0:T(8,128)(2,1)}, u32[]{:S(2)}) copy-start(bf16[1,1,256,256]{3,2,1,0:T(8,128)(2,1)} %l_hbm.1) | copy-start | bytes 393220
  10.4 0.9 %copy-start.7 = (bf16[1,1,256,256]{3,2,1,0:T(8,128)(2,1)S(1)}, bf16[1,1,256,256]{3,2,1,0:T(8,128)(2,1)}, u32[]{:S(2)}) copy-start(bf16[1,1,256,256]{3,2,1,0:T(8,128)(2,1)} %u_hbm.1) | copy-start | bytes 393220
  11.3 0.7 %copy-start.8 = (s32[1,8]{1,0:T(1,128)S(1)}, s32[1,8]{1,0:T(1,128)}, u32[]{:S(2)}) copy-start(s32[1,8]{1,0:T(1,128)} %l_ids_hbm.1) | copy-start | bytes 100
  11.9 0.7 %copy-start.9 = (s32[1,8]{1,0:T(1,128)S(1)}, s32[1,8]{1,0:T(1,128)}, u32[]{:S(2)}) copy-start(s32[1,8]{1,0:T(1,128)} %u_ids_hbm.1) | copy-start | bytes 100
  12.6 22.9 %copy-start.10 = (s32[16]{0:T(128)S(1)}, s32[16]{0:T(128)}, u32[]{:S(2)}) copy-start(s32[16]{0:T(128)} %row_order.1) | copy-start | bytes 196
  12.6 22.9 %copy-start.11 = (s32[16]{0:T(128)S(1)}, s32[16]{0:T(128)}, u32[]{:S(2)}) copy-start(s32[16]{0:T(128)} %col_order.1) | copy-start | bytes 196

commit v2 on v1

--- a/solution.py
+++ b/solution.py
@@ -304,8 +304,9 @@
         ],
         compiler_params=pltpu.CompilerParams(
             collective_id=0, has_side_effects=True, vmem_limit_bytes=28 * 2**20),
-    )(l_ids, u_ids, l_ids, u_ids, l_blocks, u_blocks, inv_upper, inv_lower,
-      front_in, leaf_lower, leaf_upper, leaf_front)
+    )(l_ids, u_ids, *(pltpu.with_memory_space_constraint(x, pltpu.HBM) for x in (
+        l_ids, u_ids, l_blocks, u_blocks, inv_upper, inv_lower, front_in, leaf_lower,
+        leaf_upper, leaf_front)))
     return pl.pallas_call(
         functools.partial(finish, (n_layer, n_row, n_col, tiles_side, inv_upper.shape[0])),
         name="finish",

time: 38.8 us -> 26 us (0.67)
  local copies, waits for them, and re-layouts: 11.9 us -> 0.01 us
  Pallas kernels: 25.8 us -> 25.2 us
    unnamed x24 -> x4, local copies, waits for them, and re-layouts: 11.9 us -> 0.01 us
    pallas_call x1, Pallas kernels: 22.9 us -> 22.1 us  [shards(): pl.pallas_call(functools.partial(exchange, (n_layer, n_row, n_col, tiles_...]
where the time goes in v2:
time: 26 us; the launch traced here: 25.9 us
  Pallas kernels  25.2 us (97%)
  between operations  0.67 us (3%)
    pallas_call x1, Pallas kernels, shards(): pl.pallas_call(functools.partial(exchange, (n_layer, n_row, n_col, tiles_...  22.1 us
    pallas_call x1, Pallas kernels, shards(): pl.pallas_call(functools.partial(finish, (n_layer, n_row, n_col, tiles_si...  3.08 us

profile of v2, /device:TPU:0, one launch (start us, length us, event | category | flops | bytes accessed | tf_op | source)
XLA Modules:
  0.0 25.9 jit_solution(13024054506420029229)
XLA Ops:
  0.6 0.0 copy-start.1
  0.6 0.0 copy-start
  0.7 22.1 %exchange.1 = (bf16[4,4,64,256]{3,2,1,0:T(8,128)(2,1)S(1)}, bf16[2,4,256,256]{3,2,1,0:T(8,128)(2,1)S(1)}, s32[4,1,8]{2,1,0:T(1,128)S(1)}, s32[4,1,8]{2,1,0:T(1,1...) custom-call(s32[1,8]{1,0:T(1,128)} %l_ids_hbm.1, s32[1,8]{1,0:T(1,128)} %u_ids_hbm.1, ...), custom_call_target="tpu_custom_call" | custom-call | tf_op jit(solution)/shard_map/exchange/pallas_call | solution.py:272
  22.8 0.0 copy-done.1
  22.8 0.0 copy-done
  22.8 3.1 %finish.1 = (f32[8,4,64,256]{3,2,1,0:T(8,128)}, bf16[1,1024,1024]{2,1,0:T(8,128)(2,1)}) custom-call(s32[4,1,8]{2,1,0:T(1,128)S(1)} %get-tuple-element.8.l_ids, s32[4,1,8]{2,1,0:T(1,128)S(1)} %get-tuple-element.9.u_ids, s32[16]{0:T(128)S(1)} %copy-done, s32[16]{0:T(128)S(1)} %copy-done.1, bf16[4,4,64,256]{3,2,1,0:T(8,128)(2,1)S(1)} %get-tuple-element.10.low_all, ...), custom_call_target="tpu_custom_call" | custom-call | tf_op jit(solution)/shard_map/finish/pallas_call | solution.py:310
Async XLA Ops:
  0.6 22.2 %copy-start.1 = (s32[16]{0:T(128)S(1)}, s32[16]{0:T(128)}, u32[]{:S(2)}) copy-start(s32[16]{0:T(128)} %col_order.1) | copy-start | bytes 196
  0.6 22.2 %copy-start = (s32[16]{0:T(128)S(1)}, s32[16]{0:T(128)}, u32[]{:S(2)}) copy-start(s32[16]{0:T(128)} %row_order.1) | copy-start | bytes 196

commit v3 on v2

--- a/solution.py
+++ b/solution.py
@@ -39,7 +39,7 @@
         (l_ids_hbm, l_ids_all.at[lay]), (u_ids_hbm, u_ids_all.at[lay]),
     ]
     local = [pltpu.make_async_copy(src, dst, loc.at[i]) for i, (src, dst) in enumerate(local)]
-    for copy in local:
+    for copy in local[:4]:
         copy.start()
 
     barrier = pltpu.get_barrier_semaphore()
@@ -155,13 +155,12 @@
         ids_copy(1, u_ids_hbm, u_ids_all, t).start()
 
     for copy in local[4:]:
-        copy.wait()
+        copy.start()
 
     for t in range(1, n_layer):
         l = layer_at(t)
         low_arrived(col, l)
         pass_on(col, l, True, True)
-    leaf(0, n_leaf // 4)
 
     for d in range(1, n_col):
         for t in range(n_layer):
@@ -177,8 +176,14 @@
                 low_arrived(col + d, l)
                 pass_on(col + d, l, False, True)
 
-        if d == 1:
-            leaf(n_leaf // 4, n_leaf)
+            step = (d - 1) * n_layer + t
+            if step == 0:
+                for copy in local[4:]:
+                    copy.wait()
+            if step < n_leaf:
+                last = n_leaf if step == (n_col - 1) * n_layer - 1 else step + 1
+                leaf(step, last)
+
         if d == max(1, n_col - 2):
             for t in range(1, n_layer):
                 l = layer_at(t)

time: 26 us -> 25.4 us (0.977)
  Pallas kernels: 25.2 us -> 24.5 us
    pallas_call x1, Pallas kernels: 22.1 us -> 21.7 us  [shards(): pl.pallas_call(functools.partial(exchange, (n_layer, n_row, n_col, tiles_...]
    pallas_call x1, Pallas kernels: 3.08 us -> 2.81 us  [shards(): pl.pallas_call(functools.partial(finish, (n_layer, n_row, n_col, tiles_si...]
where the time goes in v3:
time: 25.4 us; the launch traced here: 25.2 us
  Pallas kernels  24.5 us (96%)
  between operations  0.67 us (3%)
    pallas_call x1, Pallas kernels, shards(): pl.pallas_call(functools.partial(exchange, (n_layer, n_row, n_col, tiles_...  21.7 us
    pallas_call x1, Pallas kernels, shards(): pl.pallas_call(functools.partial(finish, (n_layer, n_row, n_col, tiles_si...  2.81 us

profile of v3, /device:TPU:0, one launch (start us, length us, event | category | flops | bytes accessed | tf_op | source)
XLA Modules:
  0.0 25.2 jit_solution(17575162854577022844)
XLA Ops:
  0.6 0.0 copy-start.1
  0.6 0.0 copy-start
  0.7 21.7 %exchange.1 = (bf16[4,4,64,256]{3,2,1,0:T(8,128)(2,1)S(1)}, bf16[2,4,256,256]{3,2,1,0:T(8,128)(2,1)S(1)}, s32[4,1,8]{2,1,0:T(1,128)S(1)}, s32[4,1,8]{2,1,0:T(1,1...) custom-call(s32[1,8]{1,0:T(1,128)} %l_ids_hbm.1, s32[1,8]{1,0:T(1,128)} %u_ids_hbm.1, ...), custom_call_target="tpu_custom_call" | custom-call | tf_op jit(solution)/shard_map/exchange/pallas_call | solution.py:277
  22.3 0.0 copy-done.1
  22.3 0.0 copy-done
  22.4 2.8 %finish.1 = (f32[8,4,64,256]{3,2,1,0:T(8,128)}, bf16[1,1024,1024]{2,1,0:T(8,128)(2,1)}) custom-call(s32[4,1,8]{2,1,0:T(1,128)S(1)} %get-tuple-element.8.l_ids, s32[4,1,8]{2,1,0:T(1,128)S(1)} %get-tuple-element.9.u_ids, s32[16]{0:T(128)S(1)} %copy-done, s32[16]{0:T(128)S(1)} %copy-done.1, bf16[4,4,64,256]{3,2,1,0:T(8,128)(2,1)S(1)} %get-tuple-element.10.low_all, ...), custom_call_target="tpu_custom_call" | custom-call | tf_op jit(solution)/shard_map/finish/pallas_call | solution.py:315
Async XLA Ops:
  0.6 21.7 %copy-start.1 = (s32[16]{0:T(128)S(1)}, s32[16]{0:T(128)}, u32[]{:S(2)}) copy-start(s32[16]{0:T(128)} %col_order.1) | copy-start | bytes 196
  0.6 21.7 %copy-start = (s32[16]{0:T(128)S(1)}, s32[16]{0:T(128)}, u32[]{:S(2)}) copy-start(s32[16]{0:T(128)} %row_order.1) | copy-start | bytes 196

commit v4 on v3

--- a/solution.py
+++ b/solution.py
@@ -100,17 +100,12 @@
     def low_arrived(s, l):
         low_copy(low_all.at[s, l], s, l, low_send.at[0], {"layer": layer_at(1)}).wait_recv()
 
-    def leaf(first, last):
+    def leaf(i):
         per = ll.shape[0] // LEAF_ROWS
-
-        def body(i, carry):
-            rows = pl.ds(pl.multiple_of(lax.rem(i, per) * LEAF_ROWS, LEAF_ROWS), LEAF_ROWS)
-            cols = pl.ds(pl.multiple_of((i // per) * LEAF_COLS, LEAF_COLS), LEAF_COLS)
-            update = jnp.dot(ll[rows, :], lu[:, cols], preferred_element_type=jnp.float32)
-            leaf_v[rows, cols] = (lf[rows, cols].astype(jnp.float32) - update).astype(leaf_v.dtype)
-            return carry
-
-        lax.fori_loop(first, last, body, 0)
+        rows = pl.ds(pl.multiple_of(lax.rem(i, per) * LEAF_ROWS, LEAF_ROWS), LEAF_ROWS)
+        cols = pl.ds(pl.multiple_of((i // per) * LEAF_COLS, LEAF_COLS), LEAF_COLS)
+        update = jnp.dot(ll[rows, :], lu[:, cols], preferred_element_type=jnp.float32)
+        leaf_v[rows, cols] = (lf[rows, cols].astype(jnp.float32) - update).astype(leaf_v.dtype)
 
     n_leaf = (ll.shape[0] // LEAF_ROWS) * (lu.shape[1] // LEAF_COLS)
     place = row * n_col + col
@@ -146,50 +141,56 @@
         inv_l[u_ids_sm[0, place] // tiles_side], u_v[...], preferred_element_type=jnp.float32
     ).astype(upper.dtype)
     up_all[row, lay] = upper[...]
-    for t in range(1, n_layer):
-        up_plane(t).start()
     for t in range(1, n_row):
         up_row(lay, t).start()
+    for copy in local[4:]:
+        copy.start()
+
+    for t in range(1, n_layer):
+        l = layer_at(t)
+        low_arrived(col, l)
+        pass_on(col, l, True, True)
+    for t in range(1, n_layer):
+        up_plane(t).start()
     for t in range(1, n_layer):
         ids_copy(0, l_ids_hbm, l_ids_all, t).start()
         ids_copy(1, u_ids_hbm, u_ids_all, t).start()
 
+    up_round = max(1, n_col - 2)
+    n_steps = (n_col - 1) * n_layer
+
+    def line_step(step, carry):
+        d = step // n_layer + 1
+        t = lax.rem(step, n_layer)
+        l = layer_at(t)
+
+        @pl.when(col - d >= 0)
+        def _():
+            low_arrived(col - d, l)
+            pass_on(col - d, l, True, False)
+
+        @pl.when(col + d < n_col)
+        def _():
+            low_arrived(col + d, l)
+            pass_on(col + d, l, False, True)
+
+        @pl.when((d == up_round) & (t > 0))
+        def _():
+            up_copy(upper, l, up_send.at[l], {"layer": l}).wait_recv()
+            for u in range(1, n_row):
+                up_row(l, u).start()
+
+        @pl.when(step < n_leaf)
+        def _():
+            leaf(step)
+
+        return carry
+
     for copy in local[4:]:
-        copy.start()
-
-    for t in range(1, n_layer):
-        l = layer_at(t)
-        low_arrived(col, l)
-        pass_on(col, l, True, True)
-
-    for d in range(1, n_col):
-        for t in range(n_layer):
-            l = layer_at(t)
-
-            @pl.when(col - d >= 0)
-            def _():
-                low_arrived(col - d, l)
-                pass_on(col - d, l, True, False)
-
-            @pl.when(col + d < n_col)
-            def _():
-                low_arrived(col + d, l)
-                pass_on(col + d, l, False, True)
-
-            step = (d - 1) * n_layer + t
-            if step == 0:
-                for copy in local[4:]:
-                    copy.wait()
-            if step < n_leaf:
-                last = n_leaf if step == (n_col - 1) * n_layer - 1 else step + 1
-                leaf(step, last)
-
-        if d == max(1, n_col - 2):
-            for t in range(1, n_layer):
-                l = layer_at(t)
-                up_copy(upper, l, up_send.at[l], {"layer": l}).wait_recv()
-                for u in range(1, n_row):
-                    up_row(l, u).start()
+        copy.wait()
+    lax.fori_loop(0, n_steps, line_step, 0)
+    for i in range(n_steps, n_leaf):
+        leaf(i)
 
     for t in range(1, n_row):
         for l in range(n_layer):

time: 25.4 us -> 23.6 us (0.929)
  Pallas kernels: 24.5 us -> 22.8 us
    pallas_call x1, Pallas kernels: 21.7 us -> 19.8 us  [shards(): pl.pallas_call(functools.partial(exchange, (n_layer, n_row, n_col, tiles_...]
where the time goes in v4:
time: 23.6 us; the launch traced here: 23.5 us
  Pallas kernels  22.8 us (97%)
  between operations  0.67 us (3%)
    pallas_call x1, Pallas kernels, shards(): pl.pallas_call(functools.partial(exchange, (n_layer, n_row, n_col, tiles_...  19.8 us
    pallas_call x1, Pallas kernels, shards(): pl.pallas_call(functools.partial(finish, (n_layer, n_row, n_col, tiles_si...  3 us

profile of v4, /device:TPU:0, one launch (start us, length us, event | category | flops | bytes accessed | tf_op | source)
XLA Modules:
  0.0 23.5 jit_solution(14960081552604917949)
XLA Ops:
  0.6 0.0 copy-start.1
  0.6 0.0 copy-start
  0.7 19.8 %exchange.1 = (bf16[4,4,64,256]{3,2,1,0:T(8,128)(2,1)S(1)}, bf16[2,4,256,256]{3,2,1,0:T(8,128)(2,1)S(1)}, s32[4,1,8]{2,1,0:T(1,128)S(1)}, s32[4,1,8]{2,1,0:T(1,1...) custom-call(s32[1,8]{1,0:T(1,128)} %l_ids_hbm.1, s32[1,8]{1,0:T(1,128)} %u_ids_hbm.1, ...), custom_call_target="tpu_custom_call" | custom-call | tf_op jit(solution)/shard_map/exchange/pallas_call | solution.py:278
  20.4 0.0 copy-done.1
  20.5 0.0 copy-done
  20.5 3.0 %finish.1 = (f32[8,4,64,256]{3,2,1,0:T(8,128)}, bf16[1,1024,1024]{2,1,0:T(8,128)(2,1)}) custom-call(s32[4,1,8]{2,1,0:T(1,128)S(1)} %get-tuple-element.8.l_ids, s32[4,1,8]{2,1,0:T(1,128)S(1)} %get-tuple-element.9.u_ids, s32[16]{0:T(128)S(1)} %copy-done, s32[16]{0:T(128)S(1)} %copy-done.1, bf16[4,4,64,256]{3,2,1,0:T(8,128)(2,1)S(1)} %get-tuple-element.10.low_all, ...), custom_call_target="tpu_custom_call" | custom-call | tf_op jit(solution)/shard_map/finish/pallas_call | solution.py:316
Async XLA Ops:
  0.6 19.8 %copy-start.1 = (s32[16]{0:T(128)S(1)}, s32[16]{0:T(128)}, u32[]{:S(2)}) copy-start(s32[16]{0:T(128)} %col_order.1) | copy-start | bytes 196
  0.6 19.8 %copy-start = (s32[16]{0:T(128)S(1)}, s32[16]{0:T(128)}, u32[]{:S(2)}) copy-start(s32[16]{0:T(128)} %row_order.1) | copy-start | bytes 196

commit v5 on v4

--- a/solution.py
+++ b/solution.py
@@ -52,13 +52,14 @@
     for t in range(1, n_row):
         greet({"row": row_at(t)})
 
-    @pl.when(col + 1 < n_col)
-    def _():
-        greet({"col": col + 1})
-
-    @pl.when(col > 0)
-    def _():
-        greet({"col": col - 1})
+    for hops in (1, 2):
+        @pl.when(col + hops < n_col)
+        def _():
+            greet({"col": col + hops})
+
+        @pl.when(col - hops >= 0)
+        def _():
+            greet({"col": col - hops})
 
     def low_copy(src, s, l, sem, device):
         return pltpu.make_async_remote_copy(
@@ -73,11 +74,13 @@
     def low_rows(l):
         return lower.at[pl.ds(pl.multiple_of(l * high, high), high)]
 
-    def right(s, l):
-        return low_copy(low_all.at[s, l], s, l, line_send.at[0, s, l], {"col": col + 1})
-
-    def left(s, l):
-        return low_copy(low_all.at[s, l], s, l, line_send.at[1, s, l], {"col": col - 1})
+    def right(s, l, hops=1):
+        sem = line_send.at[2 * hops - 2, s, l]
+        return low_copy(low_all.at[s, l], s, l, sem, {"col": col + hops})
+
+    def left(s, l, hops=1):
+        sem = line_send.at[2 * hops - 1, s, l]
+        return low_copy(low_all.at[s, l], s, l, sem, {"col": col - hops})
 
     def plane(t):
         l = layer_at(t)
@@ -112,28 +115,32 @@
 
     local[0].wait()
     local[1].wait()
+    for copy in local[4:]:
+        copy.start()
     lower[...] = jnp.dot(
         l_v[...], inv_u[l_ids_sm[0, place] % panels], preferred_element_type=jnp.float32
     ).astype(lower.dtype)
     low_all[col, lay] = low_rows(lay)[...]
 
-    on_line = (col + 1 < n_col).astype(jnp.int32) + (col > 0).astype(jnp.int32)
+    on_line = sum(
+        (col + hops < n_col).astype(jnp.int32) + (col - hops >= 0).astype(jnp.int32)
+        for hops in (1, 2))
     pl.semaphore_wait(barrier, n_layer - 1 + n_row - 1 + on_line)
 
     for t in range(1, n_layer):
         plane(t).start()
 
-    def pass_on(s, l, go_right, go_left):
-        if go_right:
-            @pl.when(col + 1 < n_col)
-            def _():
-                right(s, l).start()
-        if go_left:
-            @pl.when(col > 0)
-            def _():
-                left(s, l).start()
-
-    pass_on(col, lay, True, True)
+    def spread(l):
+        for hops in (1, 2):
+            @pl.when(col + hops < n_col)
+            def _():
+                right(col, l, hops).start()
+
+            @pl.when(col - hops >= 0)
+            def _():
+                left(col, l, hops).start()
+
+    spread(lay)
 
     local[2].wait()
     local[3].wait()
@@ -143,13 +150,10 @@
     up_all[row, lay] = upper[...]
     for t in range(1, n_row):
         up_row(lay, t).start()
-    for copy in local[4:]:
-        copy.start()
-
     for t in range(1, n_layer):
         l = layer_at(t)
         low_arrived(col, l)
-        pass_on(col, l, True, True)
+        spread(l)
     for t in range(1, n_layer):
         up_plane(t).start()
     for t in range(1, n_layer):
@@ -158,6 +162,7 @@
 
     up_round = max(1, n_col - 2)
     n_steps = (n_col - 1) * n_layer
+    leaf_from = min(2, n_steps - 1)
 
     def line_step(step, carry):
         d = step // n_layer + 1
@@ -167,12 +172,18 @@
         @pl.when(col - d >= 0)
         def _():
             low_arrived(col - d, l)
-            pass_on(col - d, l, True, False)
+
+            @pl.when((d > 1) & (col + 1 < n_col))
+            def _():
+                right(col - d, l).start()
 
         @pl.when(col + d < n_col)
         def _():
             low_arrived(col + d, l)
-            pass_on(col + d, l, False, True)
+
+            @pl.when((d > 1) & (col > 0))
+            def _():
+                left(col + d, l).start()
 
         @pl.when((d == up_round) & (t > 0))
         def _():
@@ -180,17 +191,22 @@
             for u in range(1, n_row):
                 up_row(l, u).start()
 
-        @pl.when(step < n_leaf)
-        def _():
-            leaf(step)
+        @pl.when(step == leaf_from)
+        def _():
+            for copy in local[4:7]:
+                copy.wait()
+
+        @pl.when((step >= leaf_from) & (step < leaf_from + n_leaf))
+        def _():
+            leaf(step - leaf_from)
 
         return carry
 
-    for copy in local[4:]:
+    lax.fori_loop(0, n_steps, line_step, 0)
+    for i in range(n_steps - leaf_from, n_leaf):
+        leaf(i)
+    for copy in local[7:]:
         copy.wait()
-    lax.fori_loop(0, n_steps, line_step, 0)
-    for i in range(n_steps, n_leaf):
-        leaf(i)
 
     for t in range(1, n_row):
         for l in range(n_layer):
@@ -209,15 +225,15 @@
                 src_ref=src, dst_ref=dst.at[l], send_sem=ids_send.at[which, l],
                 recv_sem=ids_recv.at[which, l], device_id={"layer": l},
                 device_id_type=MESH).wait_recv()
-    for d in range(n_col):
-        for l in range(n_layer):
-            @pl.when((col - d >= 0) & (col + 1 < n_col))
-            def _():
-                right(col - d, l).wait_send()
-
-            @pl.when((col + d < n_col) & (col > 0))
-            def _():
-                left(col + d, l).wait_send()
+    for l in range(n_layer):
+        for d, hops in [(0, 1), (0, 2)] + [(d, 1) for d in range(2, n_col)]:
+            @pl.when((col - d >= 0) & (col + hops < n_col))
+            def _():
+                right(col - d, l, hops).wait_send()
+
+            @pl.when((col + d < n_col) & (col - hops >= 0))
+            def _():
+                left(col + d, l, hops).wait_send()
 
 
 def finish(
@@ -301,7 +317,7 @@
             dma((10,)),
             dma((n_col, n_layer)),
             dma((n_layer,)),
-            dma((2, n_col, n_layer)),
+            dma((4, n_col, n_layer)),
             dma((n_row, n_layer)),
             dma((n_layer,)),
             dma((n_row, n_layer)),

time: 23.6 us -> 25.6 us (1.085)
  Pallas kernels: 22.8 us -> 24.7 us
    pallas_call x1, Pallas kernels: 19.8 us -> 21.8 us  [shards(): pl.pallas_call(functools.partial(exchange, (n_layer, n_row, n_col, tiles_...]
where the time goes in v5:
time: 25.6 us; the launch traced here: 25.4 us
  Pallas kernels  24.7 us (96%)
  between operations  0.67 us (3%)
    pallas_call x1, Pallas kernels, shards(): pl.pallas_call(functools.partial(exchange, (n_layer, n_row, n_col, tiles_...  21.8 us
    pallas_call x1, Pallas kernels, shards(): pl.pallas_call(functools.partial(finish, (n_layer, n_row, n_col, tiles_si...  2.86 us

profile of v5, /device:TPU:0, one launch (start us, length us, event | category | flops | bytes accessed | tf_op | source)
XLA Modules:
  0.0 25.4 jit_solution(13905450910609936170)
XLA Ops:
  0.6 0.0 copy-start.1
  0.6 0.0 copy-start
  0.7 21.8 %exchange.1 = (bf16[4,4,64,256]{3,2,1,0:T(8,128)(2,1)S(1)}, bf16[2,4,256,256]{3,2,1,0:T(8,128)(2,1)S(1)}, s32[4,1,8]{2,1,0:T(1,128)S(1)}, s32[4,1,8]{2,1,0:T(1,1...) custom-call(s32[1,8]{1,0:T(1,128)} %l_ids_hbm.1, s32[1,8]{1,0:T(1,128)} %u_ids_hbm.1, ...), custom_call_target="tpu_custom_call" | custom-call | tf_op jit(solution)/shard_map/exchange/pallas_call | solution.py:294
  22.5 0.0 copy-done.1
  22.5 0.0 copy-done
  22.5 2.9 %finish.1 = (f32[8,4,64,256]{3,2,1,0:T(8,128)}, bf16[1,1024,1024]{2,1,0:T(8,128)(2,1)}) custom-call(s32[4,1,8]{2,1,0:T(1,128)S(1)} %get-tuple-element.8.l_ids, s32[4,1,8]{2,1,0:T(1,128)S(1)} %get-tuple-element.9.u_ids, s32[16]{0:T(128)S(1)} %copy-done, s32[16]{0:T(128)S(1)} %copy-done.1, bf16[4,4,64,256]{3,2,1,0:T(8,128)(2,1)S(1)} %get-tuple-element.10.low_all, ...), custom_call_target="tpu_custom_call" | custom-call | tf_op jit(solution)/shard_map/finish/pallas_call | solution.py:332
Async XLA Ops:
  0.6 21.9 %copy-start.1 = (s32[16]{0:T(128)S(1)}, s32[16]{0:T(128)}, u32[]{:S(2)}) copy-start(s32[16]{0:T(128)} %col_order.1) | copy-start | bytes 196
  0.6 21.9 %copy-start = (s32[16]{0:T(128)S(1)}, s32[16]{0:T(128)}, u32[]{:S(2)}) copy-start(s32[16]{0:T(128)} %row_order.1) | copy-start | bytes 196

commit v6 on v4

--- a/solution.py
+++ b/solution.py
@@ -112,6 +112,8 @@
 
     local[0].wait()
     local[1].wait()
+    for copy in local[4:]:
+        copy.start()
     lower[...] = jnp.dot(
         l_v[...], inv_u[l_ids_sm[0, place] % panels], preferred_element_type=jnp.float32
     ).astype(lower.dtype)
@@ -143,9 +145,6 @@
     up_all[row, lay] = upper[...]
     for t in range(1, n_row):
         up_row(lay, t).start()
-    for copy in local[4:]:
-        copy.start()
-
     for t in range(1, n_layer):
         l = layer_at(t)
         low_arrived(col, l)
@@ -158,6 +157,7 @@
 
     up_round = max(1, n_col - 2)
     n_steps = (n_col - 1) * n_layer
+    leaf_from = min(2, n_steps - 1)
 
     def line_step(step, carry):
         d = step // n_layer + 1
@@ -180,17 +180,22 @@
             for u in range(1, n_row):
                 up_row(l, u).start()
 
-        @pl.when(step < n_leaf)
-        def _():
-            leaf(step)
+        @pl.when(step == leaf_from)
+        def _():
+            for copy in local[4:7]:
+                copy.wait()
+
+        @pl.when((step >= leaf_from) & (step < leaf_from + n_leaf))
+        def _():
+            leaf(step - leaf_from)
 
         return carry
 
-    for copy in local[4:]:
+    lax.fori_loop(0, n_steps, line_step, 0)
+    for i in range(n_steps - leaf_from, n_leaf):
+        leaf(i)
+    for copy in local[7:]:
         copy.wait()
-    lax.fori_loop(0, n_steps, line_step, 0)
-    for i in range(n_steps, n_leaf):
-        leaf(i)
 
     for t in range(1, n_row):
         for l in range(n_layer):
@@ -231,7 +236,6 @@
     rows_owned, cols_owned = acc.shape[0], acc.shape[1]
     leaf_copy = pltpu.make_async_copy(leaf_v, leaf_out.at[0], sem.at[0])
     leaf_copy.start()
-    acc[...] = front_v[...]
 
     def find(order, start, count, value):
         at = jnp.int32(0)
@@ -319,12 +323,14 @@
         out_shape=(
             jax.ShapeDtypeStruct(front_in.shape, front_in.dtype),
             jax.ShapeDtypeStruct(leaf_front.shape, bf16),
+            pltpu.VMEM(front_in.shape, front_in.dtype),
         ),
         in_specs=[smem] * 4 + [vmem] * 4,
-        out_specs=(any_, any_),
-        scratch_shapes=[pltpu.VMEM(front_in.shape, front_in.dtype), dma((2,))],
+        out_specs=(any_, any_, vmem),
+        scratch_shapes=[dma((2,))],
+        input_output_aliases={6: 2},
         compiler_params=pltpu.CompilerParams(vmem_limit_bytes=28 * 2**20),
-    )(l_all, u_all, row_order, col_order, low_all, up_all, front_v, leaf_v)
+    )(l_all, u_all, row_order, col_order, low_all, up_all, front_v, leaf_v)[:2]
 
 
 def solution(mesh):

time: 23.6 us -> 23.5 us (level)
  Pallas kernels: 22.8 us -> 22.5 us
    pallas_call x1, Pallas kernels: 3 us -> 2.73 us  [shards(): pl.pallas_call(functools.partial(finish, (n_layer, n_row, n_col, tiles_si...]
where the time goes in v6:
time: 23.5 us; the launch traced here: 23.2 us
  Pallas kernels  22.5 us (96%)
  between operations  0.67 us (3%)
    pallas_call x1, Pallas kernels, shards(): pl.pallas_call(functools.partial(exchange, (n_layer, n_row, n_col, tiles_...  19.8 us
    pallas_call x1, Pallas kernels, shards(): pl.pallas_call(functools.partial(finish, (n_layer, n_row, n_col, tiles_si...  2.73 us

profile of v6, /device:TPU:0, one launch (start us, length us, event | category | flops | bytes accessed | tf_op | source)
XLA Modules:
  0.0 23.2 jit_solution(9423766660911493782)
XLA Ops:
  0.6 0.0 copy-start.1
  0.6 0.0 copy-start
  0.7 19.8 %exchange.1 = (bf16[4,4,64,256]{3,2,1,0:T(8,128)(2,1)S(1)}, bf16[2,4,256,256]{3,2,1,0:T(8,128)(2,1)S(1)}, s32[4,1,8]{2,1,0:T(1,128)S(1)}, s32[4,1,8]{2,1,0:T(1,1...) custom-call(s32[1,8]{1,0:T(1,128)} %l_ids_hbm.1, s32[1,8]{1,0:T(1,128)} %u_ids_hbm.1, ...), custom_call_target="tpu_custom_call" | custom-call | tf_op jit(solution)/shard_map/exchange/pallas_call | solution.py:282
  20.4 0.0 copy-done.1
  20.5 0.0 copy-done
  20.5 2.7 %finish.1 = (f32[8,4,64,256]{3,2,1,0:T(8,128)}, bf16[1,1024,1024]{2,1,0:T(8,128)(2,1)}, f32[8,4,64,256]{3,2,1,0:T(8,128)S(1)}) custom-call(s32[4,1,8]{2,1,0:T(1,128)S(1)} %get-tuple-element.10.l_ids, s32[4,1,8]{2,1,0:T(1,128)S(1)} %get-tuple-element.11.u_ids, s32[16]{0:T(128)S(1)} %copy-done, s32[16]{0:T(128)S(1)} %copy-done.1, ...), custom_call_target="tpu_custom_call", output_to_operand_aliasing={{2}: (6, {})} | custom-call | tf_op jit(solution)/shard_map/finish/pallas_call | solution.py:320
Async XLA Ops:
  0.6 19.8 %copy-start.1 = (s32[16]{0:T(128)S(1)}, s32[16]{0:T(128)}, u32[]{:S(2)}) copy-start(s32[16]{0:T(128)} %col_order.1) | copy-start | bytes 196
  0.6 19.8 %copy-start = (s32[16]{0:T(128)S(1)}, s32[16]{0:T(128)}, u32[]{:S(2)}) copy-start(s32[16]{0:T(128)} %row_order.1) | copy-start | bytes 196

commit v7 on v6

--- a/solution.py
+++ b/solution.py
@@ -39,9 +39,6 @@
         (l_ids_hbm, l_ids_all.at[lay]), (u_ids_hbm, u_ids_all.at[lay]),
     ]
     local = [pltpu.make_async_copy(src, dst, loc.at[i]) for i, (src, dst) in enumerate(local)]
-    for copy in local[:4]:
-        copy.start()
-
     barrier = pltpu.get_barrier_semaphore()
 
     def greet(device):
@@ -59,6 +56,9 @@
     @pl.when(col > 0)
     def _():
         greet({"col": col - 1})
+
+    for copy in local[:2]:
+        copy.start()
 
     def low_copy(src, s, l, sem, device):
         return pltpu.make_async_remote_copy(
@@ -112,7 +112,7 @@
 
     local[0].wait()
     local[1].wait()
-    for copy in local[4:]:
+    for copy in local[2:4]:
         copy.start()
     lower[...] = jnp.dot(
         l_v[...], inv_u[l_ids_sm[0, place] % panels], preferred_element_type=jnp.float32
@@ -139,6 +139,8 @@
 
     local[2].wait()
     local[3].wait()
+    for copy in local[4:]:
+        copy.start()
     upper[...] = jnp.dot(
         inv_l[u_ids_sm[0, place] // tiles_side], u_v[...], preferred_element_type=jnp.float32
     ).astype(upper.dtype)
@@ -155,7 +157,8 @@
         ids_copy(0, l_ids_hbm, l_ids_all, t).start()
         ids_copy(1, u_ids_hbm, u_ids_all, t).start()
 
-    up_round = max(1, n_col - 2)
+    inner = (col > 0) & (col + 1 < n_col)
+    up_round = jnp.where(inner, n_col - 1, max(1, n_col - 2))
     n_steps = (n_col - 1) * n_layer
     leaf_from = min(2, n_steps - 1)
 

time: 23.5 us -> 23.6 us (level)
  no operation moved by 1% of the time
where the time goes in v7:
time: 23.6 us; the launch traced here: 23.1 us
  Pallas kernels  22.4 us (95%)
  between operations  0.67 us (3%)
    pallas_call x1, Pallas kernels, shards(): pl.pallas_call(functools.partial(exchange, (n_layer, n_row, n_col, tiles_...  19.8 us
    pallas_call x1, Pallas kernels, shards(): pl.pallas_call(functools.partial(finish, (n_layer, n_row, n_col, tiles_si...  2.64 us

profile of v7, /device:TPU:0, one launch (start us, length us, event | category | flops | bytes accessed | tf_op | source)
XLA Modules:
  0.0 23.1 jit_solution(18141373399917549836)
XLA Ops:
  0.6 0.0 copy-start.1
  0.6 0.0 copy-start
  0.7 19.8 %exchange.1 = (bf16[4,4,64,256]{3,2,1,0:T(8,128)(2,1)S(1)}, bf16[2,4,256,256]{3,2,1,0:T(8,128)(2,1)S(1)}, s32[4,1,8]{2,1,0:T(1,128)S(1)}, s32[4,1,8]{2,1,0:T(1,1...) custom-call(s32[1,8]{1,0:T(1,128)} %l_ids_hbm.1, s32[1,8]{1,0:T(1,128)} %u_ids_hbm.1, ...), custom_call_target="tpu_custom_call" | custom-call | tf_op jit(solution)/shard_map/exchange/pallas_call | solution.py:285
  20.4 0.0 copy-done.1
  20.5 0.0 copy-done
  20.5 2.6 %finish.1 = (f32[8,4,64,256]{3,2,1,0:T(8,128)}, bf16[1,1024,1024]{2,1,0:T(8,128)(2,1)}, f32[8,4,64,256]{3,2,1,0:T(8,128)S(1)}) custom-call(s32[4,1,8]{2,1,0:T(1,128)S(1)} %get-tuple-element.10.l_ids, s32[4,1,8]{2,1,0:T(1,128)S(1)} %get-tuple-element.11.u_ids, s32[16]{0:T(128)S(1)} %copy-done, s32[16]{0:T(128)S(1)} %copy-done.1, ...), custom_call_target="tpu_custom_call", output_to_operand_aliasing={{2}: (6, {})} | custom-call | tf_op jit(solution)/shard_map/finish/pallas_call | solution.py:323
Async XLA Ops:
  0.6 19.8 %copy-start.1 = (s32[16]{0:T(128)S(1)}, s32[16]{0:T(128)}, u32[]{:S(2)}) copy-start(s32[16]{0:T(128)} %col_order.1) | copy-start | bytes 196
  0.6 19.8 %copy-start = (s32[16]{0:T(128)S(1)}, s32[16]{0:T(128)}, u32[]{:S(2)}) copy-start(s32[16]{0:T(128)} %row_order.1) | copy-start | bytes 196

commit v8 on v7

--- a/solution.py
+++ b/solution.py
@@ -167,6 +167,13 @@
         t = lax.rem(step, n_layer)
         l = layer_at(t)
 
+        @pl.when((d == up_round) & (t < n_layer - 1))
+        def _():
+            peer = layer_at(t + 1)
+            up_copy(upper, peer, up_send.at[peer], {"layer": peer}).wait_recv()
+            for u in range(1, n_row):
+                up_row(peer, u).start()
+
         @pl.when(col - d >= 0)
         def _():
             low_arrived(col - d, l)
@@ -176,12 +183,6 @@
         def _():
             low_arrived(col + d, l)
             pass_on(col + d, l, False, True)
-
-        @pl.when((d == up_round) & (t > 0))
-        def _():
-            up_copy(upper, l, up_send.at[l], {"layer": l}).wait_recv()
-            for u in range(1, n_row):
-                up_row(l, u).start()
 
         @pl.when(step == leaf_from)
         def _():

time: 23.6 us -> 23.4 us (level); the launches traced: 23.1 us -> 23.2 us
  no operation moved by 1% of the time
where the time goes in v8:
time: 23.4 us; the launch traced here: 23.2 us
  Pallas kernels  22.6 us (97%)
  between operations  0.67 us (3%)
    pallas_call x1, Pallas kernels, shards(): pl.pallas_call(functools.partial(exchange, (n_layer, n_row, n_col, tiles_...  19.8 us
    pallas_call x1, Pallas kernels, shards(): pl.pallas_call(functools.partial(finish, (n_layer, n_row, n_col, tiles_si...  2.76 us

profile of v8, /device:TPU:0, one launch (start us, length us, event | category | flops | bytes accessed | tf_op | source)
XLA Modules:
  0.0 23.2 jit_solution(5973858297131831080)
XLA Ops:
  0.6 0.0 copy-start.1
  0.6 0.0 copy-start
  0.7 19.8 %exchange.1 = (bf16[4,4,64,256]{3,2,1,0:T(8,128)(2,1)S(1)}, bf16[2,4,256,256]{3,2,1,0:T(8,128)(2,1)S(1)}, s32[4,1,8]{2,1,0:T(1,128)S(1)}, s32[4,1,8]{2,1,0:T(1,1...) custom-call(s32[1,8]{1,0:T(1,128)} %l_ids_hbm.1, s32[1,8]{1,0:T(1,128)} %u_ids_hbm.1, ...), custom_call_target="tpu_custom_call" | custom-call | tf_op jit(solution)/shard_map/exchange/pallas_call | solution.py:286
  20.5 0.0 copy-done.1
  20.5 0.0 copy-done
  20.5 2.8 %finish.1 = (f32[8,4,64,256]{3,2,1,0:T(8,128)}, bf16[1,1024,1024]{2,1,0:T(8,128)(2,1)}, f32[8,4,64,256]{3,2,1,0:T(8,128)S(1)}) custom-call(s32[4,1,8]{2,1,0:T(1,128)S(1)} %get-tuple-element.10.l_ids, s32[4,1,8]{2,1,0:T(1,128)S(1)} %get-tuple-element.11.u_ids, s32[16]{0:T(128)S(1)} %copy-done, s32[16]{0:T(128)S(1)} %copy-done.1, ...), custom_call_target="tpu_custom_call", output_to_operand_aliasing={{2}: (6, {})} | custom-call | tf_op jit(solution)/shard_map/finish/pallas_call | solution.py:324
Async XLA Ops:
  0.6 19.8 %copy-start.1 = (s32[16]{0:T(128)S(1)}, s32[16]{0:T(128)}, u32[]{:S(2)}) copy-start(s32[16]{0:T(128)} %col_order.1) | copy-start | bytes 196
  0.6 19.8 %copy-start = (s32[16]{0:T(128)S(1)}, s32[16]{0:T(128)}, u32[]{:S(2)}) copy-start(s32[16]{0:T(128)} %row_order.1) | copy-start | bytes 196
